TPU v7x, 32 devices: a whole 2x2x4 slice. The times are simulated.
32 devices in a mesh: row: 4 (over y, x), col: 8 (over z, core).
Axes of the slice: x: 2, y: 2, z: 4, core: 2. Of those that a mesh axis runs over, the one named last changes fastest.
Arguments:
- points: int32 [16, 3, 1024], P('row', None, 'col'), may hold values from 0 to 31
- ranks: int32 [16], replicated, may hold values from 64 to 256, as said below
- bases: bfloat16 [16, 1024, 256], P('row', 'col'), may hold values from -0.375 to 0.375
- pivots: bfloat16 [2, 256, 256], replicated, may hold values from -0.119628906 to 0.119628906
- probes: bfloat16 [16, 64, 1024], P('col'), may hold values from -0.119628906 to 0.119628906
Outputs:
- updated: bfloat16 [16, 16, 256, 256], P('row', 'col')
- images: float32 [16, 64, 1024], P('row', None, 'col')
Inputs may be any that keep to these rules, and one draw needn't show every extreme that they name: `ranks`: the rank of each tile; some tile has rank 256 and some rank 256 // 4.
All inputs are finite; a program needn't handle non-finite values.
Results may differ from a plain program's by a relative error of at most 0.004.
The roundings to bfloat16 on the way count: a program that leaves them out, or rounds other values in their place, can miss the bound.
Values may be sent and summed in bfloat16 or wider, within the bound.
A program may use at most 64 MiB of HBM per device.

v0:
```python
import jax
import jax.numpy as jnp
from jax import lax
from jax.sharding import PartitionSpec as P

B = 1024
R = 256
PANELS = 2


nugget = 0.25
decay_length = 4.0
wave_length = 3.0


def spread(x, axis, root):
    mine = lax.axis_index(axis) == root
    return lax.psum(jnp.where(mine, x, jnp.zeros_like(x)), axis)


def kernel_block(rows, cols):
    diff = rows[:, :, None] - cols[:, None, :]
    dist = jnp.sqrt(jnp.sum(diff * diff, axis=0) + nugget)
    return (jnp.exp(-dist / decay_length) * jnp.cos(dist / wave_length)).astype(jnp.bfloat16)


def body(points, ranks, bases, pivots, probes):
    row_count = bases.shape[0]
    col_count = probes.shape[0]
    row_index = lax.axis_index("row")
    col_index = lax.axis_index("col")
    row_bases, row_points = (
        lax.all_gather(bases, "col", axis=1, tiled=True),
        lax.all_gather(points.astype(jnp.bfloat16), "col", axis=2, tiled=True),
    )
    root = col_index * col_count // row_count
    offset = col_index * col_count - root * row_count
    picked_bases = lax.dynamic_slice_in_dim(row_bases, offset, col_count, 0)
    picked_points = lax.dynamic_slice_in_dim(row_points, offset, col_count, 0)
    col_bases, col_points = (spread(picked_bases, "row", root), spread(picked_points, "row", root))
    col_coords = col_points.astype(jnp.float32)
    block = min(B, 256)
    nblocks = B // block

    def row_tile(item):
        tile_points, tile_bases = item
        coords = tile_points.astype(jnp.float32).reshape(3, nblocks, block).transpose(1, 0, 2)
        basis_blocks = tile_bases.reshape(nblocks, block, R)

        def add_block(total, blk):
            block_points, block_bases = blk
            tiles = jax.vmap(lambda other: kernel_block(block_points, other))(col_coords)
            proj = jnp.einsum(
                "jnm,jmr->jnr", tiles, col_bases, preferred_element_type=jnp.float32
            ).astype(jnp.bfloat16)
            return (
                total
                + jnp.einsum("nr,jns->jrs", block_bases, proj, preferred_element_type=jnp.float32),
                None,
            )

        total, _ = lax.scan(
            add_block, jnp.zeros((col_count, R, R), jnp.float32), (coords, basis_blocks)
        )
        return total

    raw = lax.map(row_tile, (row_points, row_bases))
    rank_iota = jnp.arange(R, dtype=jnp.int32)
    row_ranks = lax.dynamic_slice_in_dim(ranks, row_index * row_count, row_count)
    col_ranks = lax.dynamic_slice_in_dim(ranks, col_index * col_count, col_count)
    row_mask = (rank_iota[None, :] < row_ranks[:, None]).astype(jnp.float32)
    col_mask = (rank_iota[None, :] < col_ranks[:, None]).astype(jnp.float32)
    cores = (raw * row_mask[:, None, :, None] * col_mask[None, :, None, :]).astype(jnp.bfloat16)
    row_panel = spread(cores, "col", 0)
    col_panel = spread(cores[:PANELS], "row", 0)
    left = jnp.einsum(
        "ikab,kbc->ikac", row_panel, pivots, preferred_element_type=jnp.float32
    ).astype(jnp.bfloat16)
    update = jnp.einsum("ikac,kjcd->ijad", left, col_panel, preferred_element_type=jnp.float32)
    row_ids = row_index * row_count + jnp.arange(row_count, dtype=jnp.int32)
    col_ids = col_index * col_count + jnp.arange(col_count, dtype=jnp.int32)
    trailing = (row_ids >= PANELS)[:, None] & (col_ids >= PANELS)[None, :]
    updated = (
        cores.astype(jnp.float32) - jnp.where(trailing[:, :, None, None], update, 0.0)
    ).astype(jnp.bfloat16)
    probe_cores = jnp.einsum(
        "jpn,jnr->jpr", probes, col_bases, preferred_element_type=jnp.float32
    ).astype(jnp.bfloat16)
    partial_cores = jnp.einsum(
        "ijab,jpb->ipa", updated, probe_cores, preferred_element_type=jnp.float32
    )
    summed = lax.psum(partial_cores, "col")
    images = jnp.einsum(
        "ipa,ina->ipn", summed, bases.astype(jnp.float32), precision=lax.Precision.HIGHEST
    )
    return (updated, images)


def solution(mesh):
    placed = (P("row", None, "col"), P(), P("row", "col", None), P(), P("col", None, None))
    return jax.shard_map(
        body,
        mesh=mesh,
        in_specs=placed,
        out_specs=(P("row", "col", None, None), P("row", None, "col")),
        check_vma=False,
    )
```

profile of v0, /device:TPU:7, one launch (start us, length us, event | category | flops | bytes accessed | tf_op | source)
XLA Modules:
  0.0 440.8 jit_solution(3983174135087618088)
XLA Ops:
  7.2 0.7 all-gather.2.cloned.1.call-update
  8.0 32.4 %all-gather.2.cloned.1.call-done = bf16[4,1024,256]{2,1,0:T(8,128)(2,1)} async-done(((bf16[4,128,256]{2,1,0:T(8,128)(2,1)}), bf16[4,1024,256]{2,1,0:T(8,128)(2,1)}) %all-gather.2.cloned.1.call-update) | async-done | bytes 2097168 | tf_op jit(solution)/shard_map/all_gather | solution.py:33
  40.4 2.3 dynamic-slice_select_fusion
  42.7 10.5 %all_gather.6 = bf16[4,3,1024]{2,0,1:T(4,128)(2,1)S(1)} all-gather(bf16[4,3,128]{2,0,1:T(4,128)(2,1)S(1)} %convert_element_type.53), channel_id=1, replica_groups=mesh['row'=4,'col'=8] {'col'}, dimensions={2}, use_global_device_ids=true | all-gather | bytes 27648 | tf_op jit(solution)/shard_map/all_gather | solution.py:34
  53.3 9.8 %psum.35 = bf16[2,3,1024]{2,0,1:T(2,128)(2,1)S(1)} all-reduce(bf16[2,3,1024]{2,0,1:T(2,128)(2,1)S(1)} %broadcast_select_fusion.1), channel_id=1, replica_groups=mesh['row'=4,'col'=8] {'row'}, use_global_device_ids=true, to_apply=%region_0.1 | all-reduce | flops 6144 | bytes 24576 | tf_op jit(solution)/shard_map/psum | solution.py:18
  63.4 31.5 %all-reduce.5.cloned.1.call-done = bf16[2,1024,256]{2,1,0:T(8,128)(2,1)} async-done(((bf16[2,1024,256]{2,1,0:T(8,128)(2,1)}), bf16[2,1024,256]{2,1,0:T(8,128)(2,1)}) %all-reduce.5.cloned.1.call-update) | async-done | bytes 1048592 | tf_op jit(solution)/shard_map/psum | solution.py:18
  94.9 168.2 %while.25 = (s32[]{:T(128)}, f32[4,2,256,256]{3,2,1,0:T(8,128)}, bf16[4,3,1024]{2,1,0:T(4,128)(2,1)S(1)}, bf16[4,1024,256]{2,1,0:T(8,128)(2,1)}, f32[2,3,1024]{2...) while((s32[]{:T(128)}, f32[4,2,256,256]{3,2,1,0:T(8,128)}, ...), condition=%wide.region_6.7_spmd.clone, body=%wide.region_2.6_spmd.sunk.clone | while | flops 343280640 | bytes 9633548 | solution.py:67
  94.9 1.1 constant_dynamic-slice_fusion.7
  96.0 39.9 %while.24 = (s32[]{:T(128)}, f32[2,256,256]{1,2,0:T(8,128)S(1)}, f32[4,3,256]{2,1,0:T(4,128)S(1)}, f32[2,3,1024]{2,1,0:T(4,128)S(1)}, bf16[2,1024,256]{2,1,0:T(8...) while((s32[]{:T(128)}, f32[2,256,256]{1,2,0:T(8,128)S(1)}, ...), condition=%wide.region_5.5_spmd.clone, body=%wide.region_3.4_spmd.clone.sunk | while | flops 343277568 | bytes 6456423 | solution.py:62
  96.0 0.7 multiply_reduce_fusion.2
  96.7 9.3 %fusion.31 = f32[2,256,256]{1,2,0:T(8,128)S(1)} fusion(bf16[2,1024,256]{2,1,0:T(8,128)(2,1)} %get-tuple-element.269, f32[2,256,1024]{2,1,0:T(8,128)S(1)} %multiply_reduce_fusion.2, f32[2,256,256]{1,2,0:T(8,128)S(1)} %get-tuple-element.258, pred[]{:T(512)S(6)} %compare.5, bf16[4,256,256]{2,1,0:T(8,128)(2,1)S(1)} %get-tuple-element.270, ...), kind=kOutput, calls=%fused_computation.3.clone.1 | convolution fusion | flops 339083264 | bytes 4325381 | tf_op jit(solution)/shard_map/while/body/eval_jaxpr/while/body/eval_jaxpr/nr,jns->jrs/dot_general | solution.py:58
  106.0 0.7 multiply_reduce_fusion.2
  106.7 9.3 %fusion.31 = f32[2,256,256]{1,2,0:T(8,128)S(1)} fusion(bf16[2,1024,256]{2,1,0:T(8,128)(2,1)} %get-tuple-element.269, f32[2,256,1024]{2,1,0:T(8,128)S(1)} %multiply_reduce_fusion.2, f32[2,256,256]{1,2,0:T(8,128)S(1)} %get-tuple-element.258, pred[]{:T(512)S(6)} %compare.5, bf16[4,256,256]{2,1,0:T(8,128)(2,1)S(1)} %get-tuple-element.270, ...), kind=kOutput, calls=%fused_computation.3.clone.1 | convolution fusion | flops 339083264 | bytes 4325381 | tf_op jit(solution)/shard_map/while/body/eval_jaxpr/while/body/eval_jaxpr/nr,jns->jrs/dot_general | solution.py:58
  116.0 0.7 multiply_reduce_fusion.2
  116.6 9.3 %fusion.31 = f32[2,256,256]{1,2,0:T(8,128)S(1)} fusion(bf16[2,1024,256]{2,1,0:T(8,128)(2,1)} %get-tuple-element.269, f32[2,256,1024]{2,1,0:T(8,128)S(1)} %multiply_reduce_fusion.2, f32[2,256,256]{1,2,0:T(8,128)S(1)} %get-tuple-element.258, pred[]{:T(512)S(6)} %compare.5, bf16[4,256,256]{2,1,0:T(8,128)(2,1)S(1)} %get-tuple-element.270, ...), kind=kOutput, calls=%fused_computation.3.clone.1 | convolution fusion | flops 339083264 | bytes 4325381 | tf_op jit(solution)/shard_map/while/body/eval_jaxpr/while/body/eval_jaxpr/nr,jns->jrs/dot_general | solution.py:58
  125.9 0.7 multiply_reduce_fusion.2
  126.6 9.3 %fusion.31 = f32[2,256,256]{1,2,0:T(8,128)S(1)} fusion(bf16[2,1024,256]{2,1,0:T(8,128)(2,1)} %get-tuple-element.269, f32[2,256,1024]{2,1,0:T(8,128)S(1)} %multiply_reduce_fusion.2, f32[2,256,256]{1,2,0:T(8,128)S(1)} %get-tuple-element.258, pred[]{:T(512)S(6)} %compare.5, bf16[4,256,256]{2,1,0:T(8,128)(2,1)S(1)} %get-tuple-element.270, ...), kind=kOutput, calls=%fused_computation.3.clone.1 | convolution fusion | flops 339083264 | bytes 4325381 | tf_op jit(solution)/shard_map/while/body/eval_jaxpr/while/body/eval_jaxpr/nr,jns->jrs/dot_general | solution.py:58
  135.9 0.2 copy.34
  136.1 0.8 constant_dynamic-update-slice_fusion.3
  136.9 1.1 constant_dynamic-slice_fusion.7
  138.1 39.9 %while.24 = (s32[]{:T(128)}, f32[2,256,256]{1,2,0:T(8,128)S(1)}, f32[4,3,256]{2,1,0:T(4,128)S(1)}, f32[2,3,1024]{2,1,0:T(4,128)S(1)}, bf16[2,1024,256]{2,1,0:T(8...) while((s32[]{:T(128)}, f32[2,256,256]{1,2,0:T(8,128)S(1)}, ...), condition=%wide.region_5.5_spmd.clone, body=%wide.region_3.4_spmd.clone.sunk | while | flops 343277568 | bytes 6456423 | solution.py:62
  138.1 0.7 multiply_reduce_fusion.2
  138.8 9.3 %fusion.31 = f32[2,256,256]{1,2,0:T(8,128)S(1)} fusion(bf16[2,1024,256]{2,1,0:T(8,128)(2,1)} %get-tuple-element.269, f32[2,256,1024]{2,1,0:T(8,128)S(1)} %multiply_reduce_fusion.2, f32[2,256,256]{1,2,0:T(8,128)S(1)} %get-tuple-element.258, pred[]{:T(512)S(6)} %compare.5, bf16[4,256,256]{2,1,0:T(8,128)(2,1)S(1)} %get-tuple-element.270, ...), kind=kOutput, calls=%fused_computation.3.clone.1 | convolution fusion | flops 339083264 | bytes 4325381 | tf_op jit(solution)/shard_map/while/body/eval_jaxpr/while/body/eval_jaxpr/nr,jns->jrs/dot_general | solution.py:58
  148.1 0.7 multiply_reduce_fusion.2
  148.7 9.3 %fusion.31 = f32[2,256,256]{1,2,0:T(8,128)S(1)} fusion(bf16[2,1024,256]{2,1,0:T(8,128)(2,1)} %get-tuple-element.269, f32[2,256,1024]{2,1,0:T(8,128)S(1)} %multiply_reduce_fusion.2, f32[2,256,256]{1,2,0:T(8,128)S(1)} %get-tuple-element.258, pred[]{:T(512)S(6)} %compare.5, bf16[4,256,256]{2,1,0:T(8,128)(2,1)S(1)} %get-tuple-element.270, ...), kind=kOutput, calls=%fused_computation.3.clone.1 | convolution fusion | flops 339083264 | bytes 4325381 | tf_op jit(solution)/shard_map/while/body/eval_jaxpr/while/body/eval_jaxpr/nr,jns->jrs/dot_general | solution.py:58
  158.0 0.7 multiply_reduce_fusion.2
  158.7 9.3 %fusion.31 = f32[2,256,256]{1,2,0:T(8,128)S(1)} fusion(bf16[2,1024,256]{2,1,0:T(8,128)(2,1)} %get-tuple-element.269, f32[2,256,1024]{2,1,0:T(8,128)S(1)} %multiply_reduce_fusion.2, f32[2,256,256]{1,2,0:T(8,128)S(1)} %get-tuple-element.258, pred[]{:T(512)S(6)} %compare.5, bf16[4,256,256]{2,1,0:T(8,128)(2,1)S(1)} %get-tuple-element.270, ...), kind=kOutput, calls=%fused_computation.3.clone.1 | convolution fusion | flops 339083264 | bytes 4325381 | tf_op jit(solution)/shard_map/while/body/eval_jaxpr/while/body/eval_jaxpr/nr,jns->jrs/dot_general | solution.py:58
  168.0 0.7 multiply_reduce_fusion.2
  168.7 9.3 %fusion.31 = f32[2,256,256]{1,2,0:T(8,128)S(1)} fusion(bf16[2,1024,256]{2,1,0:T(8,128)(2,1)} %get-tuple-element.269, f32[2,256,1024]{2,1,0:T(8,128)S(1)} %multiply_reduce_fusion.2, f32[2,256,256]{1,2,0:T(8,128)S(1)} %get-tuple-element.258, pred[]{:T(512)S(6)} %compare.5, bf16[4,256,256]{2,1,0:T(8,128)(2,1)S(1)} %get-tuple-element.270, ...), kind=kOutput, calls=%fused_computation.3.clone.1 | convolution fusion | flops 339083264 | bytes 4325381 | tf_op jit(solution)/shard_map/while/body/eval_jaxpr/while/body/eval_jaxpr/nr,jns->jrs/dot_general | solution.py:58
  177.9 0.2 copy.34
  178.1 0.9 constant_dynamic-update-slice_fusion.3
  179.0 1.1 constant_dynamic-slice_fusion.7
  180.1 39.9 %while.24 = (s32[]{:T(128)}, f32[2,256,256]{1,2,0:T(8,128)S(1)}, f32[4,3,256]{2,1,0:T(4,128)S(1)}, f32[2,3,1024]{2,1,0:T(4,128)S(1)}, bf16[2,1024,256]{2,1,0:T(8...) while((s32[]{:T(128)}, f32[2,256,256]{1,2,0:T(8,128)S(1)}, ...), condition=%wide.region_5.5_spmd.clone, body=%wide.region_3.4_spmd.clone.sunk | while | flops 343277568 | bytes 6456423 | solution.py:62
  180.1 0.7 multiply_reduce_fusion.2
  180.8 9.3 %fusion.31 = f32[2,256,256]{1,2,0:T(8,128)S(1)} fusion(bf16[2,1024,256]{2,1,0:T(8,128)(2,1)} %get-tuple-element.269, f32[2,256,1024]{2,1,0:T(8,128)S(1)} %multiply_reduce_fusion.2, f32[2,256,256]{1,2,0:T(8,128)S(1)} %get-tuple-element.258, pred[]{:T(512)S(6)} %compare.5, bf16[4,256,256]{2,1,0:T(8,128)(2,1)S(1)} %get-tuple-element.270, ...), kind=kOutput, calls=%fused_computation.3.clone.1 | convolution fusion | flops 339083264 | bytes 4325381 | tf_op jit(solution)/shard_map/while/body/eval_jaxpr/while/body/eval_jaxpr/nr,jns->jrs/dot_general | solution.py:58
  190.1 0.7 multiply_reduce_fusion.2
  190.8 9.3 %fusion.31 = f32[2,256,256]{1,2,0:T(8,128)S(1)} fusion(bf16[2,1024,256]{2,1,0:T(8,128)(2,1)} %get-tuple-element.269, f32[2,256,1024]{2,1,0:T(8,128)S(1)} %multiply_reduce_fusion.2, f32[2,256,256]{1,2,0:T(8,128)S(1)} %get-tuple-element.258, pred[]{:T(512)S(6)} %compare.5, bf16[4,256,256]{2,1,0:T(8,128)(2,1)S(1)} %get-tuple-element.270, ...), kind=kOutput, calls=%fused_computation.3.clone.1 | convolution fusion | flops 339083264 | bytes 4325381 | tf_op jit(solution)/shard_map/while/body/eval_jaxpr/while/body/eval_jaxpr/nr,jns->jrs/dot_general | solution.py:58
  200.1 0.7 multiply_reduce_fusion.2
  200.7 9.3 %fusion.31 = f32[2,256,256]{1,2,0:T(8,128)S(1)} fusion(bf16[2,1024,256]{2,1,0:T(8,128)(2,1)} %get-tuple-element.269, f32[2,256,1024]{2,1,0:T(8,128)S(1)} %multiply_reduce_fusion.2, f32[2,256,256]{1,2,0:T(8,128)S(1)} %get-tuple-element.258, pred[]{:T(512)S(6)} %compare.5, bf16[4,256,256]{2,1,0:T(8,128)(2,1)S(1)} %get-tuple-element.270, ...), kind=kOutput, calls=%fused_computation.3.clone.1 | convolution fusion | flops 339083264 | bytes 4325381 | tf_op jit(solution)/shard_map/while/body/eval_jaxpr/while/body/eval_jaxpr/nr,jns->jrs/dot_general | solution.py:58
  210.0 0.7 multiply_reduce_fusion.2
  210.7 9.3 %fusion.31 = f32[2,256,256]{1,2,0:T(8,128)S(1)} fusion(bf16[2,1024,256]{2,1,0:T(8,128)(2,1)} %get-tuple-element.269, f32[2,256,1024]{2,1,0:T(8,128)S(1)} %multiply_reduce_fusion.2, f32[2,256,256]{1,2,0:T(8,128)S(1)} %get-tuple-element.258, pred[]{:T(512)S(6)} %compare.5, bf16[4,256,256]{2,1,0:T(8,128)(2,1)S(1)} %get-tuple-element.270, ...), kind=kOutput, calls=%fused_computation.3.clone.1 | convolution fusion | flops 339083264 | bytes 4325381 | tf_op jit(solution)/shard_map/while/body/eval_jaxpr/while/body/eval_jaxpr/nr,jns->jrs/dot_general | solution.py:58
  220.0 0.2 copy.34
  220.2 0.8 constant_dynamic-update-slice_fusion.3
  221.0 1.1 constant_dynamic-slice_fusion.7
  222.2 39.9 %while.24 = (s32[]{:T(128)}, f32[2,256,256]{1,2,0:T(8,128)S(1)}, f32[4,3,256]{2,1,0:T(4,128)S(1)}, f32[2,3,1024]{2,1,0:T(4,128)S(1)}, bf16[2,1024,256]{2,1,0:T(8...) while((s32[]{:T(128)}, f32[2,256,256]{1,2,0:T(8,128)S(1)}, ...), condition=%wide.region_5.5_spmd.clone, body=%wide.region_3.4_spmd.clone.sunk | while | flops 343277568 | bytes 6456423 | solution.py:62
  222.2 0.7 multiply_reduce_fusion.2
  222.8 9.3 %fusion.31 = f32[2,256,256]{1,2,0:T(8,128)S(1)} fusion(bf16[2,1024,256]{2,1,0:T(8,128)(2,1)} %get-tuple-element.269, f32[2,256,1024]{2,1,0:T(8,128)S(1)} %multiply_reduce_fusion.2, f32[2,256,256]{1,2,0:T(8,128)S(1)} %get-tuple-element.258, pred[]{:T(512)S(6)} %compare.5, bf16[4,256,256]{2,1,0:T(8,128)(2,1)S(1)} %get-tuple-element.270, ...), kind=kOutput, calls=%fused_computation.3.clone.1 | convolution fusion | flops 339083264 | bytes 4325381 | tf_op jit(solution)/shard_map/while/body/eval_jaxpr/while/body/eval_jaxpr/nr,jns->jrs/dot_general | solution.py:58
  232.1 0.7 multiply_reduce_fusion.2
  232.8 9.3 %fusion.31 = f32[2,256,256]{1,2,0:T(8,128)S(1)} fusion(bf16[2,1024,256]{2,1,0:T(8,128)(2,1)} %get-tuple-element.269, f32[2,256,1024]{2,1,0:T(8,128)S(1)} %multiply_reduce_fusion.2, f32[2,256,256]{1,2,0:T(8,128)S(1)} %get-tuple-element.258, pred[]{:T(512)S(6)} %compare.5, bf16[4,256,256]{2,1,0:T(8,128)(2,1)S(1)} %get-tuple-element.270, ...), kind=kOutput, calls=%fused_computation.3.clone.1 | convolution fusion | flops 339083264 | bytes 4325381 | tf_op jit(solution)/shard_map/while/body/eval_jaxpr/while/body/eval_jaxpr/nr,jns->jrs/dot_general | solution.py:58
  242.1 0.7 multiply_reduce_fusion.2
  242.8 9.3 %fusion.31 = f32[2,256,256]{1,2,0:T(8,128)S(1)} fusion(bf16[2,1024,256]{2,1,0:T(8,128)(2,1)} %get-tuple-element.269, f32[2,256,1024]{2,1,0:T(8,128)S(1)} %multiply_reduce_fusion.2, f32[2,256,256]{1,2,0:T(8,128)S(1)} %get-tuple-element.258, pred[]{:T(512)S(6)} %compare.5, bf16[4,256,256]{2,1,0:T(8,128)(2,1)S(1)} %get-tuple-element.270, ...), kind=kOutput, calls=%fused_computation.3.clone.1 | convolution fusion | flops 339083264 | bytes 4325381 | tf_op jit(solution)/shard_map/while/body/eval_jaxpr/while/body/eval_jaxpr/nr,jns->jrs/dot_general | solution.py:58
  252.1 0.7 multiply_reduce_fusion.2
  252.8 9.3 %fusion.31 = f32[2,256,256]{1,2,0:T(8,128)S(1)} fusion(bf16[2,1024,256]{2,1,0:T(8,128)(2,1)} %get-tuple-element.269, f32[2,256,1024]{2,1,0:T(8,128)S(1)} %multiply_reduce_fusion.2, f32[2,256,256]{1,2,0:T(8,128)S(1)} %get-tuple-element.258, pred[]{:T(512)S(6)} %compare.5, bf16[4,256,256]{2,1,0:T(8,128)(2,1)S(1)} %get-tuple-element.270, ...), kind=kOutput, calls=%fused_computation.3.clone.1 | convolution fusion | flops 339083264 | bytes 4325381 | tf_op jit(solution)/shard_map/while/body/eval_jaxpr/while/body/eval_jaxpr/nr,jns->jrs/dot_general | solution.py:58
  262.0 0.2 copy.34
  262.2 0.8 constant_dynamic-update-slice_fusion.3
  263.1 3.0 broadcast_select_fusion
  266.0 0.8 slice_select_fusion
  266.9 0.5 all-reduce.9.cloned.1.call-update
  267.6 44.6 %all-reduce.7.cloned.1.call-done = bf16[2,2,256,256]{3,2,1,0:T(8,128)(2,1)} async-done(((bf16[2,2,256,256]{3,2,1,0:T(8,128)(2,1)}), bf16[2,2,256,256]{3,2,1,0:T(8,128)(2,1)}) %all-reduce.7.cloned.1.call-update) | async-done | bytes 524304 | tf_op jit(solution)/shard_map/psum | solution.py:18
  312.2 60.9 %all-reduce.9.cloned.1.call-done = bf16[4,2,256,256]{3,2,1,0:T(8,128)(2,1)} async-done(((bf16[4,2,256,256]{3,2,1,0:T(8,128)(2,1)}), bf16[4,2,256,256]{3,2,1,0:T(8,128)(2,1)}) %all-reduce.9.cloned.1.call-update) | async-done | bytes 1048592 | tf_op jit(solution)/shard_map/psum | solution.py:18
  373.1 2.4 fusion.11
  375.5 2.6 convolution_bitcast_fusion.1
  378.1 54.2 %all-reduce.11.cloned.1.call-done = f32[4,64,256]{2,1,0:T(8,128)} async-done(((f32[4,64,256]{2,1,0:T(8,128)}), f32[4,64,256]{2,1,0:T(8,128)}) %all-reduce.11.cloned.1.call-update) | async-done | bytes 262160 | tf_op jit(solution)/shard_map/psum | solution.py:92
  432.3 2.0 fusion.18
  (60 shorter events, 0.9 us)
Async XLA Ops:
  7.2 365.9 %copy-start = (bf16[2,256,256]{2,1,0:T(8,128)(2,1)S(1)}, bf16[2,256,256]{2,1,0:T(8,128)(2,1)}, u32[]{:S(2)}) copy-start(bf16[2,256,256]{2,1,0:T(8,128)(2,1)} %param.12) | copy-start | bytes 786436
  7.2 35.5 %copy-start.4 = (s32[4,3,128]{2,0,1:T(4,128)S(1)}, s32[4,3,128]{2,0,1:T(4,128)}, u32[]{:S(2)}) copy-start(s32[4,3,128]{2,0,1:T(4,128)} %param.9) | copy-start | bytes 18436
  7.2 55.9 %copy-start.5 = (s32[16]{0:T(128)S(1)}, s32[16]{0:T(128)}, u32[]{:S(2)}) copy-start(s32[16]{0:T(128)} %param.10) | copy-start | bytes 196
  7.2 33.2 %all-gather.2.cloned.1.call-start = ((), (), s32[]{:S(2)}) async-start(), calls=%async_computation | async-start | bytes 2359296 | tf_op jit(solution)/shard_map/all_gather | solution.py:33
  7.9 86.9 %all-reduce.5.cloned.1.call-start = ((), (), s32[]{:S(2)}) async-start(), calls=%async_computation.1 | async-start | bytes 2097152 | tf_op jit(solution)/shard_map/psum | solution.py:18
  42.6 269.6 %all-reduce.7.cloned.1.call-start = ((), (), s32[]{:S(2)}) async-start(), calls=%async_computation.2 | async-start | bytes 1048576 | tf_op jit(solution)/shard_map/psum | solution.py:18
  266.9 106.2 %all-reduce.9.cloned.1.call-start = ((), (), s32[]{:S(2)}) async-start(), calls=%async_computation.3 | async-start | bytes 2097152 | tf_op jit(solution)/shard_map/psum | solution.py:18
  267.5 164.8 %all-reduce.11.cloned.1.call-start = ((), (), s32[]{:S(2)}) async-start(), calls=%async_computation.4 | async-start | bytes 524288 | tf_op jit(solution)/shard_map/psum | solution.py:92
  267.6 107.8 %copy-start.1 = (bf16[2,1024,256]{2,1,0:T(8,128)(2,1)S(1)}, bf16[2,1024,256]{2,1,0:T(8,128)(2,1)}, u32[]{:S(2)}) copy-start(bf16[2,1024,256]{2,1,0:T(8,128)(2,1)} %get-tuple-element.313) | copy-start | bytes 3145732
  375.5 58.8 %copy-start.2 = (bf16[4,2,256,256]{3,2,1,0:T(8,128)(2,1)}, bf16[4,2,256,256]{3,2,1,0:T(8,128)(2,1)S(1)}, u32[]{:S(2)}) copy-start(bf16[4,2,256,256]{3,2,1,0:T(8,128)(2,1)S(1)} %fusion.11) | copy-start | bytes 3145732
  375.5 56.8 %copy-start.3 = (bf16[4,128,256]{2,1,0:T(8,128)(2,1)S(1)}, bf16[4,128,256]{2,1,0:T(8,128)(2,1)}, u32[]{:S(2)}) copy-start(bf16[4,128,256]{2,1,0:T(8,128)(2,1)} %param.11) | copy-start | bytes 786436
Sparse Core Ops, SparseCore 0:
  9.6 30.6 all-gather.1
  44.0 50.8 all-reduce.4
  267.0 45.1 all-reduce.6
  315.0 58.0 all-reduce.8
  378.2 54.0 all-reduce.10
where the time goes:
time: 445 us; the launch traced here: 441 us
  waiting for transfers between devices  225 us (51%)
  matrix products  155 us (35%)
  blocking collectives  20.3 us (5%)
  other arithmetic  16.8 us (4%)
  between operations  13.9 us (3%)
  local copies, waits for them, and re-layouts  8.84 us (2%)
    dot_general x16, matrix products, add_block(): jnp.einsum('nr,jns->jrs', block_bases, proj, preferred_element_type=jnp.f...  148 us
    psum x3, waiting for transfers between devices, spread(): return lax.psum(jnp.where(mine, x, jnp.zeros_like(x)), axis)  137 us
    psum x1, waiting for transfers between devices, body(): summed = lax.psum(partial_cores, 'col')  54.2 us
    all_gather x1, waiting for transfers between devices, body(): lax.all_gather(bases, 'col', axis=1, tiled=True)  32.4 us
    reduce_sum x16, other arithmetic, kernel_block(): dist = jnp.sqrt(jnp.sum(diff * diff, axis=0) + nugget)  10.5 us
    all_gather x1, blocking collectives, body(): lax.all_gather(points.astype(jnp.bfloat16), 'col', axis=2, tiled=True)  10.5 us
    psum x1, blocking collectives, spread(): return lax.psum(jnp.where(mine, x, jnp.zeros_like(x)), axis)  9.85 us
  transfers between devices with their start and end apart: 5, of which 5 were waited for; matrix products, arithmetic and copies ran while one was open for 0% of the time, Pallas kernels for 0%

commit v1 on v0

v1 whole, which is shorter than its diff:
```python
import functools
import math

import jax
import jax.numpy as jnp
import numpy as np
from jax import lax
from jax.experimental import pallas as pl
from jax.experimental.pallas import tpu as pltpu
from jax.sharding import PartitionSpec as P

PANELS = 2
NUGGET = 0.25
DECAY = 4.0
WAVE = 3.0
FEATS = 16
BLK = 256
SPLIT = 32
LAG = 2
GROUPS = 2


def cosine_terms(count):
    k = np.arange(64)
    u = 0.125 * (1.0 + np.cos(np.pi * (k + 0.5) / 64))
    fit = np.polynomial.chebyshev.Chebyshev.fit(
        u, np.cos(2 * np.pi * np.sqrt(u)), count - 1, domain=[0.0, 0.25]
    )
    return [float(v) for v in fit.convert(kind=np.polynomial.Polynomial).coef]


COS = cosine_terms(7)


def mixer():
    m = np.zeros((FEATS, FEATS), np.float32)
    for a in range(3):
        m[a, a] = -2.0
    m[5, 3] = m[5, 4] = 1.0
    m[3, 5] = m[4, 6] = 1.0
    m[5, 6] = NUGGET
    return m


def covariance(s):
    dist = s * lax.rsqrt(s)
    turns = dist * (1.0 / (2.0 * math.pi * WAVE))
    g = turns - jnp.round(turns)
    u = g * g
    c = COS[-1] * u + COS[-2]
    for v in COS[-3::-1]:
        c = c * u + v
    return (jnp.exp(dist * (-1.0 / DECAY)) * c).astype(jnp.bfloat16)


def xor(a, b, bits):
    return sum(((a // (1 << k) + b // (1 << k)) % 2) * (1 << k) for k in range(bits))


def kernel(
    n_row, n_col, points, ranks, bases, pivots, probes, mix,
    updated, images,
    fslot, tfull, tcol, lhs, rowb, colb, kmat, cores, rowp, colp, probec, part, rsbuf, total,
    f_s, f_r, t_s, t_r, b_s, rel_s, b_r, cl_s, c_s, c_r, rp_s, rp_r, cp_s, cp_r, rs_s, rs_r, ag_s, ag_r,
):
    nt_row, chunk, rank = bases.shape
    nt_col = probes.shape[0]
    size = probes.shape[2]
    tiles = nt_row * nt_col
    bits = n_row.bit_length() - 1
    nz = n_col // 2
    r = lax.axis_index("row")
    c = lax.axis_index("col")
    core = c % 2
    z = c // 2
    sib = z * 2 + (1 - core)
    per = nt_row // nt_col
    root = c // per
    off = (c - root * per) * nt_col

    def ring_place(v):
        out = v
        for k in range(1, bits):
            out = xor(out, v // (1 << k), bits)
        return out

    def ring_owner(v):
        return xor(v, v // 2, bits)

    q = ring_place(r)
    after = ring_owner((q + 1) % n_row)
    before = ring_owner((q + n_row - 1) % n_row)
    d = (q + n_row - ring_place(root)) % n_row
    dx = xor(r, root, bits)
    f32 = jnp.float32

    def copy(src, dst, ss, rs, row=None, col=None):
        return pltpu.make_async_remote_copy(
            src_ref=src, dst_ref=dst, send_sem=ss, recv_sem=rs,
            device_id=(r if row is None else row, c if col is None else col),
            device_id_type=pl.DeviceIdType.MESH,
        )

    barrier = pltpu.get_barrier_semaphore()
    for k in range(1, n_col):
        pl.semaphore_signal(barrier, inc=1, device_id=(r, (c + k) % n_col), device_id_type=pl.DeviceIdType.MESH)
    for k in range(1, n_row):
        pl.semaphore_signal(barrier, inc=1, device_id=((r + k) % n_row, c), device_id_type=pl.DeviceIdType.MESH)
    pl.semaphore_wait(barrier, n_col + n_row - 2)

    place = lax.broadcasted_iota(jnp.int32, (FEATS, chunk), 0)
    for i in range(nt_row):
        p = points[i]
        norm = p[0:1] * p[0:1] + p[1:2] * p[1:2] + p[2:3] * p[2:3]
        low = norm & 31
        value = jnp.where((place == 5) | (place == 6), 1, 0)
        for row, v in enumerate((p[0:1], p[1:2], p[2:3], norm - low, low)):
            value = jnp.where(place == row, v, value)
        fslot[c, i] = value.astype(f32).astype(jnp.bfloat16)

    def feat_copy(k):
        return copy(fslot.at[c], fslot.at[c], f_s.at[k], f_r.at[c], col=(c + k) % n_col)

    for k in range(1, n_col):
        feat_copy(k).start()

    def mine(slot):
        return rowb.at[:, pl.ds(pl.multiple_of(slot * chunk, chunk), chunk), :]

    def base_copy(m):
        return copy(bases, mine(c), b_s.at[m], b_r.at[c], col=((z + m) % nz) * 2 + core)

    sib_copy = copy(bases, mine(c), b_s.at[0], b_r.at[c], col=sib)

    def relay_copy(m):
        slot = ((z + m) % nz) * 2 + core
        return copy(mine(slot), mine(slot), rel_s.at[m], b_r.at[slot], col=sib)

    for m in range(1, nz):
        base_copy(m).start()
    sib_copy.start()
    rowb[:, pl.ds(pl.multiple_of(c * chunk, chunk), chunk), :] = bases[...]

    for k in range(1, n_col):
        slot = (c + k) % n_col
        copy(fslot.at[slot], fslot.at[slot], f_s.at[k], f_r.at[slot], col=slot).wait_recv()
    for k in range(n_col):
        tfull[:, :, k * chunk:(k + 1) * chunk] = fslot[k]

    def tcol_copy(k):
        return copy(tcol, tcol, t_s.at[k], t_r, row=(r + k) % n_row)

    @pl.when(d == 0)
    def _():
        for j in range(nt_col):
            tcol[j] = tfull[off + j]
        for k in range(1, n_row):
            tcol_copy(k).start()

    for i in range(nt_row):
        lhs[i] = lax.dot_general(
            tfull[i], mix[...], (((0,), (0,)), ((), ())), preferred_element_type=f32
        ).astype(jnp.bfloat16)

    @pl.when(d != 0)
    def _():
        tcol_copy(1).wait_recv()

    nblk = size // BLK

    def k_step(n, _):
        t = n // nblk
        rows = pl.ds(pl.multiple_of((n % nblk) * BLK, BLK), BLK)
        s = jnp.dot(lhs[t // nt_col, rows, :], tcol[t % nt_col], preferred_element_type=f32)
        kmat[t, rows, :] = covariance(s)
        return 0

    def run(a, b):
        lax.fori_loop(a, b, k_step, 0)

    span = 2 * chunk

    def piece(m, j):
        rows = pl.ds(pl.multiple_of(((z + m) % nz) * span, span), span)
        return colb.at[j, rows, :], rows

    def piece_copy(m, j, b):
        ref, _ = piece(m, j)
        return copy(ref, ref, c_s.at[m, j, b], c_r.at[m, j], row=xor(r, 1 << b, bits))

    def has_child(j, b):
        if j % 2 == 0:
            return dx < (1 << b)
        return dx % (2 << b) == 0

    def forward(m, go):
        for j in range(nt_col):
            for b in range(bits):
                @pl.when(has_child(j, b))
                def _():
                    if go:
                        piece_copy(m, j, b).start()
                    else:
                        piece_copy(m, j, b).wait_send()

    def root_piece(m):
        @pl.when(dx == 0)
        def _():
            for j in range(nt_col):
                ref, rows = piece(m, j)
                local = pltpu.make_async_copy(rowb.at[off + j, rows, :], ref, cl_s.at[m, j])
                local.start()
                local.wait()
            forward(m, True)

    def other_piece(m):
        @pl.when(dx != 0)
        def _():
            for j in range(nt_col):
                piece_copy(m, j, 0).wait_recv()
            forward(m, True)

    def wait_slot(slot):
        copy(bases, mine(slot), b_s.at[0], b_r.at[slot], col=sib).wait_recv()

    marks = [SPLIT * (k + 1) // (nz + 1) for k in range(nz + 1)]
    done = 0
    for m in range(nz + 1):
        run(done, marks[m])
        done = marks[m]
        if m + 1 < nz:
            wait_slot(((z + m + 1) % nz) * 2 + core)
            relay_copy(m + 1).start()
        if m < nz:
            wait_slot(((z + m) % nz) * 2 + (1 - core))
            root_piece(m)
        if m >= 1:
            other_piece(m - 1)

    for j in range(nt_col):
        probec[j] = jnp.dot(probes[j], colb[j], preferred_element_type=f32).astype(jnp.bfloat16)

    def chain_copy(t, k=1):
        return copy(rowp.at[t], rowp.at[t], rp_s.at[k, t], rp_r.at[t], col=((z + k) % nz) * 2)

    def pair_copy(t):
        return copy(rowp.at[t], rowp.at[t], rp_s.at[0, t], rp_r.at[t], col=z * 2 + 1)

    def colp_copy(t, k=1):
        return copy(colp.at[t], colp.at[t], cp_s.at[k, t], cp_r.at[t], row=(r + k) % n_row)

    def pass_on(t):
        @pl.when(c != 0)
        def _():
            chain_copy(t).wait_recv()

        @pl.when(core == 0)
        def _():
            pair_copy(t).start()

            @pl.when(z == 0)
            def _():
                for k in range(1, nz):
                    chain_copy(t, k).start()

    def tile_step(t, _):
        i = t // nt_col
        j = t % nt_col
        extra = nblk * tiles - SPLIT
        lax.fori_loop(SPLIT + t * extra // tiles, SPLIT + (t + 1) * extra // tiles, k_step, 0)
        proj = jnp.dot(kmat[t], colb[j], preferred_element_type=f32).astype(jnp.bfloat16)
        raw = lax.dot_general(rowb[i], proj, (((0,), (0,)), ((), ())), preferred_element_type=f32)
        down = lax.broadcasted_iota(jnp.int32, (rank, rank), 0) < ranks[r * nt_row + i]
        across = lax.broadcasted_iota(jnp.int32, (rank, rank), 1) < ranks[c * nt_col + j]
        tile = jnp.where(down & across, raw, 0.0).astype(jnp.bfloat16)
        cores[t] = tile

        @pl.when(jnp.logical_and(r == 0, t < PANELS * nt_col))
        def _():
            colp[t] = tile
            for k in range(1, n_row):
                colp_copy(t, k).start()

        @pl.when(c == 0)
        def _():
            rowp[t] = tile
            pass_on(t)

        @pl.when(jnp.logical_and(c != 0, t >= LAG))
        def _():
            pass_on(t - LAG)

        return 0

    lax.fori_loop(0, tiles, tile_step, 0)

    @pl.when(r != 0)
    def _():
        for t in range(PANELS * nt_col):
            colp_copy(t).wait_recv()

    count = probes.shape[1]
    group = part.shape[0] // GROUPS
    height = group // n_col

    def cut(g, slot):
        return pl.ds(pl.multiple_of(g * group + slot * height, height), height)

    def rs_copy(g, k):
        slot = (c + k) % n_col
        return copy(part.at[cut(g, slot), :], rsbuf.at[g, c], rs_s.at[g, k], rs_r.at[g, c], col=slot)

    def ag_copy(g, k):
        rows = total.at[cut(g, c), :]
        return copy(rows, rows, ag_s.at[g, k], ag_r.at[g, c], col=(c + k) % n_col)

    def update_row(i):
        lefts = [
            jnp.dot(rowp[i * PANELS + k], pivots[k], preferred_element_type=f32).astype(jnp.bfloat16)
            for k in range(PANELS)
        ]
        acc = jnp.zeros((count, rank), f32)
        for j in range(nt_col):
            change = sum(
                jnp.dot(lefts[k], colp[k * nt_col + j], preferred_element_type=f32) for k in range(PANELS)
            )
            trailing = jnp.logical_and(r * nt_row + i >= PANELS, c * nt_col + j >= PANELS)
            new = cores[i * nt_col + j].astype(f32) - jnp.where(trailing, change, 0.0)
            new = new.astype(jnp.bfloat16)
            updated[i, j] = new
            acc += lax.dot_general(probec[j], new, (((1,), (1,)), ((), ())), preferred_element_type=f32)
        part[i * count:(i + 1) * count, :] = acc

    def add_up(g):
        for k in range(1, n_col):
            slot = (c + k) % n_col
            copy(part.at[cut(g, c), :], rsbuf.at[g, slot], rs_s.at[g, k], rs_r.at[g, slot], col=slot).wait_recv()
        acc = rsbuf[g, 0]
        for k in range(1, n_col):
            acc += rsbuf[g, k]
        total[cut(g, c), :] = acc
        for k in range(1, n_col):
            ag_copy(g, k).start()

    for i in range(nt_row):
        for t in range(max(tiles - LAG, i * PANELS), min(tiles, (i + 1) * PANELS)):
            @pl.when(c != 0)
            def _():
                pass_on(t)

        update_row(i)
        if (i + 1) * GROUPS % nt_row == 0:
            g = (i + 1) * GROUPS // nt_row - 1
            for k in range(1, n_col):
                rs_copy(g, k).start()
            rsbuf[g, c] = part[cut(g, c), :]
    for g in range(GROUPS):
        add_up(g)
    for g in range(GROUPS):
        for k in range(1, n_col):
            slot = (c + k) % n_col
            rows = total.at[cut(g, slot), :]
            copy(rows, rows, ag_s.at[g, k], ag_r.at[g, slot], col=slot).wait_recv()
    for i in range(nt_row):
        images[i] = lax.dot_general(
            total[i * count:(i + 1) * count, :], bases[i].astype(f32),
            (((1,), (1,)), ((), ())), precision=lax.Precision.HIGHEST, preferred_element_type=f32,
        )

    for k in range(1, n_col):
        feat_copy(k).wait_send()
        for g in range(GROUPS):
            rs_copy(g, k).wait_send()
            ag_copy(g, k).wait_send()

    @pl.when(d == 0)
    def _():
        for k in range(1, n_row):
            tcol_copy(k).wait_send()

    for m in range(1, nz):
        base_copy(m).wait_send()
        relay_copy(m).wait_send()
    sib_copy.wait_send()
    for m in range(nz):
        forward(m, False)

    @pl.when(r == 0)
    def _():
        for t in range(PANELS * nt_col):
            for k in range(1, n_row):
                colp_copy(t, k).wait_send()

    @pl.when(core == 0)
    def _():
        for t in range(tiles):
            pair_copy(t).wait_send()

        @pl.when(z == 0)
        def _():
            for t in range(tiles):
                for k in range(1, nz):
                    chain_copy(t, k).wait_send()


def body(n_row, n_col, points, ranks, bases, pivots, probes):
    nt_row, chunk, rank = bases.shape
    nt_col, count, size = probes.shape
    tiles = nt_row * nt_col
    bf = jnp.bfloat16
    f32 = jnp.float32
    nz = n_col // 2
    rows = nt_row * count
    dma = pltpu.SemaphoreType.DMA
    vmem = pl.BlockSpec(memory_space=pltpu.VMEM)
    flops = 2 * tiles * size * rank * (size + rank)
    return pl.pallas_call(
        functools.partial(kernel, n_row, n_col),
        out_shape=(
            jax.ShapeDtypeStruct((nt_row, nt_col, rank, rank), bf),
            jax.ShapeDtypeStruct((nt_row, count, chunk), f32),
        ),
        in_specs=[vmem, pl.BlockSpec(memory_space=pltpu.SMEM)] + [vmem] * 4,
        out_specs=(vmem, vmem),
        scratch_shapes=[
            pltpu.VMEM((n_col, nt_row, FEATS, chunk), bf),
            pltpu.VMEM((nt_row, FEATS, size), bf),
            pltpu.VMEM((nt_col, FEATS, size), bf),
            pltpu.VMEM((nt_row, size, FEATS), bf),
            pltpu.VMEM((nt_row, size, rank), bf),
            pltpu.VMEM((nt_col, size, rank), bf),
            pltpu.VMEM((tiles, size, size), bf),
            pltpu.VMEM((tiles, rank, rank), bf),
            pltpu.VMEM((nt_row * PANELS, rank, rank), bf),
            pltpu.VMEM((PANELS * nt_col, rank, rank), bf),
            pltpu.VMEM((nt_col, count, rank), bf),
            pltpu.VMEM((rows, rank), f32),
            pltpu.VMEM((GROUPS, n_col, rows // n_col // GROUPS, rank), f32),
            pltpu.VMEM((rows, rank), f32),
            dma((n_col,)), dma((n_col,)),
            dma((n_row,)), dma,
            dma((nz,)), dma((nz,)), dma((n_col,)),
            dma((nz, nt_col)), dma((nz, nt_col, n_row.bit_length() - 1)), dma((nz, nt_col)),
            dma((nz, tiles)), dma((tiles,)),
            dma((n_row, PANELS * nt_col)), dma((PANELS * nt_col,)),
            dma((GROUPS, n_col)), dma((GROUPS, n_col)), dma((GROUPS, n_col)), dma((GROUPS, n_col)),
        ],
        compiler_params=pltpu.CompilerParams(
            collective_id=0, has_side_effects=True, vmem_limit_bytes=56 * 1024 * 1024
        ),
        cost_estimate=pl.CostEstimate(
            flops=flops, bytes_accessed=4 << 20, transcendentals=2 * tiles * size * size
        ),
    )(points, ranks, bases, pivots, probes, jnp.asarray(mixer(), bf))


def solution(mesh):
    placed = (P("row", None, "col"), P(), P("row", "col", None), P(), P("col", None, None))
    return jax.shard_map(
        functools.partial(body, mesh.shape["row"], mesh.shape["col"]),
        mesh=mesh,
        in_specs=placed,
        out_specs=(P("row", "col", None, None), P("row", None, "col")),
        check_vma=False,
    )
```

time: 445 us -> 110 us (0.25)
  waiting for transfers between devices: 225 us -> 0 us
  matrix products: 155 us -> 0 us
  Pallas kernels: 0 us -> 105 us
  blocking collectives: 20.3 us -> 0 us
  other arithmetic: 16.8 us -> 0 us
  between operations: 13.9 us -> 0.65 us
  local copies, waits for them, and re-layouts: 8.84 us -> 4.25 us
    psum x4 -> x0, waiting for transfers between devices: 191 us -> none  [the longest x3 137 us: spread(): return lax.psum(jnp.where(mine, x, jnp.zeros_like(x)), axis)]
    dot_general x19 -> x0, matrix products: 155 us -> none  [the longest x16 148 us: add_block(): jnp.einsum('nr,jns->jrs', block_bases, proj, preferred_element_type=jnp.f...]
    pallas_call x0 -> x1, Pallas kernels: none -> 105 us  [body(): pl.pallas_call(functools.partial(kernel, n_row, n_col), out_shape=(jax.Sh...]
    all_gather x1 -> x0, waiting for transfers between devices: 32.4 us -> none  [body(): lax.all_gather(bases, 'col', axis=1, tiled=True)]
    reduce_sum x16 -> x0, other arithmetic: 10.5 us -> none  [kernel_block(): dist = jnp.sqrt(jnp.sum(diff * diff, axis=0) + nugget)]
    all_gather x1 -> x0, blocking collectives: 10.5 us -> none  [body(): lax.all_gather(points.astype(jnp.bfloat16), 'col', axis=2, tiled=True)]
    psum x1 -> x0, blocking collectives: 9.85 us -> none  [spread(): return lax.psum(jnp.where(mine, x, jnp.zeros_like(x)), axis)]
    select_n x4 -> x0, other arithmetic: 6.09 us -> none  [spread(): return lax.psum(jnp.where(mine, x, jnp.zeros_like(x)), axis)]
  transfers between devices with their start and end apart: 5 -> 0, of which waited for: 5 -> 0; matrix products, arithmetic and copies ran while one was open for 0% -> 0% of each run, Pallas kernels for 0% -> 0%
where the time goes in v1:
time: 110 us
  Pallas kernels  105 us (95%)
  local copies, waits for them, and re-layouts  4.25 us (4%)
    pallas_call x1, Pallas kernels, body(): pl.pallas_call(functools.partial(kernel, n_row, n_col), out_shape=(jax.Sh...  105 us
    unnamed x5, local copies, waits for them, and re-layouts  4.25 us

profile of v1, /device:TPU:7, one launch (start us, length us, event | category | flops | bytes accessed | tf_op | source)
XLA Modules:
  0.0 110.2 jit_solution(346903985155880226)
XLA Ops:
  0.6 1.3 %copy.8.points = s32[4,3,128]{2,1,0:T(4,128)} copy(s32[4,3,128]{2,0,1:T(4,128)} %param.6) | data formatting | bytes 12288 | tf_op args[0]
  1.9 105.3 %shard_map.77 = (bf16[4,2,256,256]{3,2,1,0:T(8,128)(2,1)}, f32[4,64,128]{2,1,0:T(8,128)}) custom-call(s32[4,3,128]{2,1,0:T(4,128)} %copy.8.points, s32[16]{0:T(128)} %ranks.1, bf16[4,128,256]{2,1,0:T(8,128)(2,1)} %bases.1, bf16[2,256,256]{2,1,0:T(8,128)(2,1)} %pivots.1, bf16[2,64,1024]{2,1,0:T(8,128)(2,1)} %probes.1, bf16[16,16]{1,0:T(8,128)(2,1)} %constant.2.clone.mix), custom_call_target="tpu_custom_call" | custom-call | flops 5368709120 | bytes 4194304 | tf_op jit(solution)/shard_map/pallas_call | solution.py:417
  107.2 0.0 copy-start
  107.2 2.3 %copy.11 = bf16[4,2,256,256]{3,2,1,0:T(8,128)(2,1)} copy(bf16[4,2,256,256]{3,2,1,0:T(8,128)(2,1)} %get-tuple-element.4) | data formatting | bytes 2097152
  109.5 0.0 copy-done
  109.5 0.7 copy.12
Async XLA Ops:
  107.2 2.3 %copy-start = (f32[4,64,128]{2,1,0:T(8,128)S(1)}, f32[4,64,128]{2,1,0:T(8,128)}, u32[]{:S(2)}) copy-start(f32[4,64,128]{2,1,0:T(8,128)} %get-tuple-element.5) | copy-start | bytes 393220
